TPU v7x, 128 devices: a whole 4x4x4 slice. The times are simulated.
128 devices in a mesh: ha: 128 (over y, x, z, core).
Axes of the slice: x: 4, y: 4, z: 4, core: 2. Of those that a mesh axis runs over, the one named last changes fastest.
Arguments:
- density: float32 [4096, 18432], P('ha'), may hold values from -6 to 6
- up_link: int32 [4096, 40], P('ha'), may hold values from -1 to 4095, as said below
- down_link: int32 [4096, 40], P('ha'), may hold values from -1 to 4095, as said below
- occupation: int32 [4096, 40], P('ha'), may hold values from 0 to 3, as said below
- pigments: int32 [40], replicated, may hold values from 0 to 95
- hamiltonian: float32 [96, 96], replicated, as said below
- dipole: float32 [96, 96], replicated, as said below
- damping_rates: float32 [40], replicated, may hold values from 0.05 to 0.5
- coupling_re: float32 [40], replicated, may hold values from 0.3 to 1.5
- coupling_im: float32 [40], replicated, may hold values from -1 to 1
- field: float32 [64], replicated, may hold values from -1.5 to 1.5
- pulse_steps: int32 [2], replicated, may hold values from 0 to 63
Outputs:
- evolved: float32 [4096, 18432], P('ha')
Inputs may be any that keep to these rules, and one draw needn't show every extreme that they name: The auxiliaries are the occupation vectors over the 40 modes whose occupations sum to at most 3: in a fixed order of the modes, the first 4096 of them taken by total occupation and then lexicographically. The p-th of them lies on device sigma(p mod 128), at a slot of that device, with sigma a permutation of the devices; the slots and the labels of the modes are permuted as well. up_link[a, k] is the auxiliary with occupation of mode k raised by one if that one is among them, else -1 (always -1 where the total is 3). `down_link`: the auxiliary with occupation of mode k lowered by one, -1 where that occupation is 0; the inverse of up_link. `occupation`: each row sums to at most 3. `hamiltonian`: Symmetric, diagonal energies of order one and off-diagonal couplings. `dipole`: Symmetric.
All inputs are finite; a program needn't handle non-finite values.
Results may differ from a plain program's by a relative error of at most 0.0003.
Values sent between devices are 32-bit elements; how exact they have to be, the bound alone decides.
No kernel may reach another device: no remote copies, remote signals or barrier semaphores. Data moves between devices by JAX's collectives and lax.ppermute only.
A program may use at most 128 MiB of HBM per device.

v0:
```python
import jax
import jax.numpy as jnp
import numpy as np
from jax import lax
from jax.sharding import PartitionSpec as P

DEPTH = 3


step_length = 0.1


def canon_links(modes, depth, count):
    tiers = [np.full((1, depth), modes, np.int64)]
    for level in range(1, depth + 1):
        previous = tiers[-1]
        if level > 1:
            latest = previous[:, level - 2]
        else:
            latest = np.zeros(previous.shape[0], np.int64)
        extra = np.tile(np.arange(modes, dtype=np.int64), previous.shape[0])
        repeated = np.repeat(previous, modes, axis=0)
        keep = extra >= np.repeat(latest, modes)
        grown = repeated[keep].copy()
        grown[:, level - 1] = extra[keep]
        tiers.append(grown)
    members = np.concatenate(tiers, axis=0)[:count]
    radix = modes + 1
    powers = radix ** np.arange(depth, dtype=np.int64)
    lookup = np.full(radix**depth, -1, np.int64)
    lookup[np.sum(members * powers, axis=1)] = np.arange(count, dtype=np.int64)
    filled = np.sum(members < modes, axis=1)
    rows_all = np.arange(count)
    up_table = np.full((count, modes), -1, np.int64)
    down_table = np.full((count, modes), -1, np.int64)
    for mode in range(modes):
        holds = np.sum(members == mode, axis=1)
        added = members.copy()
        added[rows_all, np.minimum(filled, depth - 1)] = mode
        added = np.sort(added, axis=1)
        up_table[:, mode] = np.where(filled < depth, lookup[np.sum(added * powers, axis=1)], -1)
        removed = members.copy()
        removed[rows_all, np.argmax(members == mode, axis=1)] = modes
        removed = np.sort(removed, axis=1)
        down_table[:, mode] = np.where(holds > 0, lookup[np.sum(removed * powers, axis=1)], -1)
    return (up_table, down_table)


def link_capacity(modes, depth, aux_local, devices):
    count = aux_local * devices
    up_table, down_table = canon_links(modes, depth, count)
    tally = np.zeros(devices * devices, np.int64)
    source = np.repeat(np.arange(count) % devices, modes)
    for table in (up_table, down_table):
        flat = table.reshape(-1)
        live = flat >= 0
        pairs = source[live] * devices + flat[live] % devices
        tally = tally + np.bincount(pairs, minlength=devices * devices)
    return int(max(int(tally.max()), 1))


def serve(state, codes, width):
    valid = codes > 0
    flat = jnp.maximum(codes - 1, 0)
    slot = flat // width
    pig = flat % width
    rows = state[slot, pig, :]
    col_re = state[slot, :, pig]
    col_im = state[slot, :, pig + width]
    message = jnp.concatenate([rows, col_re, col_im], axis=-1)
    return jnp.where(valid[..., None], message, jnp.float32(0.0))


def derivative(state, hmat, up_msg, down_msg, level, rates, coup_re, coup_im, onehot, width):
    count = state.shape[0]
    high = lax.Precision.HIGHEST
    left = jnp.einsum("ij,ajk->aik", hmat, state, precision=high)
    right = jnp.einsum(
        "aipj,jk->aipk", state.reshape(count, width, 2, width), hmat, precision=high
    ).reshape(count, width, 2 * width)
    d_re = left[..., width:] - right[..., width:]
    d_im = right[..., :width] - left[..., :width]
    lvl = level.astype(jnp.float32)
    decay = jnp.sum(lvl * rates[None, :], axis=1)[:, None, None]
    ur_re = up_msg[..., :width]
    ur_im = up_msg[..., width : 2 * width]
    uc_re = up_msg[..., 2 * width : 3 * width]
    uc_im = up_msg[..., 3 * width :]
    pr_re = down_msg[..., :width]
    pr_im = down_msg[..., width : 2 * width]
    pc_re = down_msg[..., 2 * width : 3 * width]
    pc_im = down_msg[..., 3 * width :]
    scale_a = (lvl * coup_re[None, :])[..., None]
    scale_b = (lvl * coup_im[None, :])[..., None]
    row_re = ur_im + scale_a * pr_im + scale_b * pr_re
    col_re = -uc_im - scale_a * pc_im + scale_b * pc_re
    row_im = -ur_re - scale_a * pr_re + scale_b * pr_im
    col_im = uc_re + scale_a * pc_re + scale_b * pc_im
    d_re = (
        d_re
        + jnp.einsum("km,akj->amj", onehot, row_re, precision=high)
        + jnp.einsum("aki,km->aim", col_re, onehot, precision=high)
    )
    d_im = (
        d_im
        + jnp.einsum("km,akj->amj", onehot, row_im, precision=high)
        + jnp.einsum("aki,km->aim", col_im, onehot, precision=high)
    )
    return jnp.concatenate([d_re, d_im], axis=-1) - decay * state


def running_rank(target, devices):
    marks = (target[:, None] == jnp.arange(devices, dtype=jnp.int32)[None, :]).astype(jnp.int32)
    before = jnp.cumsum(marks, axis=0) - marks
    return jnp.sum(before * marks, axis=1)


def on_device(
    density,
    up_link,
    down_link,
    occupation,
    pigments,
    hamiltonian,
    dipole,
    damping_rates,
    coupling_re,
    coupling_im,
    field,
    pulse_steps,
):
    devices = lax.axis_size("ha")
    aux_local = density.shape[0]
    width = hamiltonian.shape[0]
    modes = pigments.shape[0]
    start = density.reshape(aux_local, width, 2 * width)
    capacity = link_capacity(modes, DEPTH, aux_local, devices)
    onehot = (pigments[:, None] == jnp.arange(width, dtype=jnp.int32)[None, :]).astype(jnp.float32)
    links = jnp.transpose(jnp.stack([up_link, down_link], axis=0), (2, 0, 1))
    valid = links >= 0
    target = jnp.where(valid, links // aux_local, devices)
    partner = jnp.where(valid, links % aux_local, 0)
    total = modes * 2 * aux_local
    flat_dest = target.reshape(total)
    ask_rank = running_rank(flat_dest, devices)
    codes_item = (partner * width + pigments[:, None, None] + 1).reshape(total)
    codes = (
        jnp.zeros((devices, capacity), jnp.int32)
        .at[flat_dest, ask_rank]
        .set(codes_item, mode="drop")
    )
    flat_valid = valid.reshape(total)
    flat_target = jnp.minimum(target.reshape(total), devices - 1)

    def neighbours(state):
        incoming = lax.all_to_all(
            serve(
                state, lax.all_to_all(codes, "ha", split_axis=0, concat_axis=0, tiled=True), width
            ),
            "ha",
            split_axis=0,
            concat_axis=0,
            tiled=True,
        )
        picked = incoming[flat_target, jnp.minimum(ask_rank, capacity - 1)]
        picked = jnp.where(flat_valid[:, None], picked, jnp.float32(0.0)).reshape(
            modes, 2, aux_local, 4 * width
        )
        return (jnp.transpose(picked[:, 0], (1, 0, 2)), jnp.transpose(picked[:, 1], (1, 0, 2)))

    def rate(state, hmat):
        up_msg, down_msg = neighbours(state)
        return derivative(
            state,
            hmat,
            up_msg,
            down_msg,
            occupation,
            damping_rates,
            coupling_re,
            coupling_im,
            onehot,
            width,
        )

    first_h = hamiltonian + field[pulse_steps[0]] * dipole
    second_h = hamiltonian + field[pulse_steps[1]] * dipole
    first = rate(start, first_h)
    middle = start + 0.5 * step_length * first
    second = rate(middle, second_h)
    return (start + step_length * second).reshape(aux_local, 2 * width * width)


def solution(mesh):
    in_specs = (
        P("ha", None),
        P("ha", None),
        P("ha", None),
        P("ha", None),
        P(),
        P(),
        P(),
        P(),
        P(),
        P(),
        P(),
        P(),
    )
    out_specs = P("ha", None)
    return jax.shard_map(
        on_device, mesh=mesh, in_specs=in_specs, out_specs=out_specs, check_vma=False
    )
```

profile of v0, /device:TPU:1, one launch (start us, length us, event | category | flops | bytes accessed | tf_op | source)
XLA Modules:
  0.0 619.7 jit_solution(9452126523126603925)
XLA Ops:
  4.4 9.9 %scatter_custom_fusion = s32[1920]{0:T(1024)S(1)} fusion(s32[2560]{0:T(1024)S(1)} %broadcast_select_fusion, s32[2560]{0:T(1024)S(1)} %reshape.313, s32[]{:T(128)} %constant.68.clone.1), kind=kCustom, calls=%fused_computation.197 | custom fusion | bytes 7684
  15.0 11.5 %all-to-all-start = ((s32[128,1,15]{2,1,0:T(1,128)}), s32[128,1,15]{2,1,0:T(1,128)S(1)}, u32[]{:S(2)}, u32[]{:S(2)}) async-start(s32[128,1,15]{2,1,0:T(1,128)} %copy.138), calls=%async_computation | async-start | bytes 131072 | tf_op jit(solution)/shard_map/all_to_all | solution.py:158
  26.5 2.7 reshape.253
  29.3 2.7 copy.144
  31.9 3.9 all-to-all-done
  36.3 76.4 %gather_fusion.2 = f32[1920,96]{1,0:T(8,128)} fusion(f32[32,96,192]{1,2,0:T(8,128)} %copy.144, s32[1920]{0:T(1024)S(1)} %reshape.275), kind=kCustom, calls=%fused_computation.2 | custom fusion | bytes 1489920 | tf_op jit(solution)/shard_map/gather | solution.py:69
  112.7 2.3 reshape.278
  115.3 79.5 %gather_fusion.1 = f32[1920,96]{1,0:T(8,128)} fusion(f32[32,96,192]{1,2,0:T(8,128)} %copy.144, s32[1920]{0:T(1024)S(1)} %reshape.269), kind=kCustom, calls=%fused_computation.1 | custom fusion | bytes 1489920 | tf_op jit(solution)/shard_map/gather | solution.py:68
  194.8 2.3 reshape.272
  197.4 19.1 %gather_fusion = f32[1920,192]{1,0:T(8,128)} fusion(f32[32,96,192]{2,1,0:T(8,128)S(1)} %reshape.253, s32[1920]{0:T(1024)S(1)} %reshape.263), kind=kCustom, calls=%fused_computation | custom fusion | bytes 2964480 | tf_op jit(solution)/shard_map/gather | solution.py:67
  216.5 2.7 reshape.266
  219.3 4.4 maximum_select_fusion
  223.8 15.2 %all-to-all-start.1 = ((f32[128,15,384]{2,1,0:T(8,128)}), f32[128,15,384]{2,1,0:T(8,128)}, u32[]{:S(2)}, u32[]{:S(2)}) async-start(f32[128,15,384]{2,1,0:T(8,128)} %maximum_select_fusion), calls=%async_computation.1 | async-start | bytes 6291456 | tf_op jit(solution)/shard_map/all_to_all | solution.py:156
  239.0 7.1 %reshape_reshape.3 = f32[32,96,2,96]{3,2,1,0:T(2,128)} reshape(f32[32,18432]{1,0:T(8,128)} %param.12) | data formatting | bytes 4718592 | tf_op jit(solution)/shard_map/reshape;reshape | solution.py:79
  250.9 9.6 %fusion.4 = f32[96,32,96,2]{2,0,3,1:T(8,128)S(1)} fusion(f32[32,96,2,96]{3,2,1,0:T(2,128)} %reshape_reshape.3, f32[96,96]{1,0:T(8,128)S(1)} %copy-done.13, f32[96,96]{1,0:T(8,128)S(1)} %copy-done.14, f32[]{:T(128)} %bitcast.1), kind=kOutput, calls=%fused_computation.20 | convolution fusion | flops 679495680 | bytes 4792324 | tf_op jit(solution)/shard_map/aipj,jk->aipk/dot_general | solution.py:78
  262.4 3.1 copy.174
  265.5 3.1 copy.173
  268.8 5.1 convolution_bitcast_fusion.1
  273.9 6.1 all-to-all-done.1
  280.0 2.8 copy.147
  282.8 29.4 %gather_fusion.3 = f32[2560,384]{1,0:T(8,128)} fusion(f32[128,15,384]{2,0,1:T(8,128)S(1)} %copy.147, s32[2560]{0:T(1024)S(1)} %get-tuple-element.18), kind=kCustom, calls=%fused_computation.3 | custom fusion | bytes 7884800 | tf_op jit(solution)/shard_map/gather | solution.py:165
  312.2 5.1 copy_select_fusion.1
  320.8 2.4 fusion.11
  323.2 2.8 fusion.13
  326.0 2.6 pad_maximum_fusion
  328.6 2.5 copy.158
  331.1 76.1 %gather_fusion.6 = f32[1920,96]{1,0:T(8,128)} fusion(f32[32,96,192]{1,2,0:T(8,128)} %copy.158, s32[1920]{0:T(1024)S(1)} %reshape.275), kind=kCustom, calls=%fused_computation.6 | custom fusion | bytes 1489920 | tf_op jit(solution)/shard_map/gather | solution.py:69
  407.3 79.3 %gather_fusion.5 = f32[1920,96]{1,0:T(8,128)} fusion(f32[32,96,192]{1,2,0:T(8,128)} %copy.158, s32[1920]{0:T(1024)S(1)} %reshape.269), kind=kCustom, calls=%fused_computation.5 | custom fusion | bytes 1489920 | tf_op jit(solution)/shard_map/gather | solution.py:68
  486.5 19.1 %gather_fusion.4 = f32[1920,192]{1,0:T(8,128)} fusion(f32[32,96,192]{2,1,0:T(8,128)S(1)} %get-tuple-element.10, s32[1920]{0:T(1024)S(1)} %reshape.263), kind=kCustom, calls=%fused_computation.4 | custom fusion | bytes 2964480 | tf_op jit(solution)/shard_map/gather | solution.py:67
  505.6 2.3 reshape.302
  507.9 2.3 reshape.296
  510.2 2.7 reshape.290
  512.9 4.3 maximum_select_fusion.1
  517.2 4.7 all-to-all-start.2
  521.9 3.9 concatenate.55
  525.8 8.5 %convolution_bitcast_fusion = f32[32,96,192]{1,2,0:T(8,128)} fusion(f32[32,96,192]{2,1,0:T(8,128)S(1)} %get-tuple-element.10, f32[96,96]{1,0:T(8,128)S(1)} %copy-done.13, f32[96,96]{1,0:T(8,128)S(1)} %copy-done.14, f32[]{:T(128)} %bitcast.32), kind=kOutput, calls=%fused_computation.28 | convolution fusion | flops 679495680 | bytes 4792324 | tf_op jit(solution)/shard_map/ij,ajk->aik/dot_general | solution.py:77
  534.3 9.4 %fusion.2 = f32[32,96,2,96]{1,3,2,0:T(8,128)} fusion(f32[96,96]{1,0:T(8,128)S(1)} %copy-done.13, f32[96,96]{1,0:T(8,128)S(1)} %copy-done.14, f32[]{:T(128)} %bitcast.32, f32[32,96,1,96]{3,1,0,2:T(8,128)S(1)} %bitcast.154, f32[32,96,1,96]{3,1,0,2:T(8,128)S(1)} %bitcast.155, f32[32,96,2,96]{3,2,1,0:T(2,128)S(1)} %copy-done.2, f32[32]{0:T(128)S(1)} %get-tuple-element.17), kind=kOutput, calls=%fused_computation.18 | convolution fusion | flops 682444800 | bytes 7151748 | tf_op jit(solution)/shard_map/aipj,jk->aipk/dot_general | solution.py:78
  543.7 19.1 %all-to-all-done.2 = f32[128,15,384]{2,1,0:T(8,128)} async-done(((f32[128,15,384]{2,1,0:T(8,128)}), f32[128,15,384]{2,1,0:T(8,128)}, u32[]{:S(2)}, u32[]{:S(2)}) %all-to-all-start.2) | async-done | bytes 2949152 | tf_op jit(solution)/shard_map/all_to_all | solution.py:156
  562.8 3.0 copy.160
  565.9 29.3 %gather_fusion.7 = f32[2560,384]{1,0:T(8,128)} fusion(f32[128,15,384]{2,0,1:T(8,128)S(1)} %copy.160, s32[2560]{0:T(1024)S(1)} %get-tuple-element.18), kind=kCustom, calls=%fused_computation.7 | custom fusion | bytes 7884800 | tf_op jit(solution)/shard_map/gather | solution.py:165
  595.2 4.8 copy_select_fusion
  600.3 2.0 fusion.23
  602.2 2.1 fusion.29
  604.4 2.0 fusion.7
  606.4 2.0 fusion.9
  608.6 2.6 copy.162
  611.2 3.8 concatenate.54
  615.0 4.5 multiply_add_fusion.1
  (91 shorter events, 13.4 us)
Async XLA Ops:
  1.9 2.0 copy-start.25
  2.0 2.1 copy-start.24
  15.0 20.8 %all-to-all-start = ((s32[128,1,15]{2,1,0:T(1,128)}), s32[128,1,15]{2,1,0:T(1,128)S(1)}, u32[]{:S(2)}, u32[]{:S(2)}) async-start(s32[128,1,15]{2,1,0:T(1,128)} %copy.138), calls=%async_computation | async-start | bytes 131072 | tf_op jit(solution)/shard_map/all_to_all | solution.py:158
  29.2 239.5 %copy-start = (f32[32,96,192]{2,1,0:T(8,128)}, f32[32,96,192]{2,1,0:T(8,128)S(1)}, u32[]{:S(2)}) copy-start(f32[32,96,192]{2,1,0:T(8,128)S(1)} %reshape.253) | copy-start | bytes 7077892
  223.8 56.2 %all-to-all-start.1 = ((f32[128,15,384]{2,1,0:T(8,128)}), f32[128,15,384]{2,1,0:T(8,128)}, u32[]{:S(2)}, u32[]{:S(2)}) async-start(f32[128,15,384]{2,1,0:T(8,128)} %maximum_select_fusion), calls=%async_computation.1 | async-start | bytes 6291456 | tf_op jit(solution)/shard_map/all_to_all | solution.py:156
  239.0 7.1 %copy-start.20 = (s32[2]{0:T(128)S(1)}, s32[2]{0:T(128)}, u32[]{:S(2)}) copy-start(s32[2]{0:T(128)} %param.23) | copy-start | bytes 28
  239.0 11.3 %copy-start.19 = (f32[64]{0:T(128)S(1)}, f32[64]{0:T(128)}, u32[]{:S(2)}) copy-start(f32[64]{0:T(128)} %param.22) | copy-start | bytes 772
  239.0 11.9 %copy-start.13 = (f32[96,96]{1,0:T(8,128)S(1)}, f32[96,96]{1,0:T(8,128)}, u32[]{:S(2)}) copy-start(f32[96,96]{1,0:T(8,128)} %param.17) | copy-start | bytes 110596
  239.0 11.9 %copy-start.14 = (f32[96,96]{1,0:T(8,128)S(1)}, f32[96,96]{1,0:T(8,128)}, u32[]{:S(2)}) copy-start(f32[96,96]{1,0:T(8,128)} %param.18) | copy-start | bytes 110596
  265.4 3.1 copy-start.15
  265.4 3.1 copy-start.16
  265.4 3.2 copy-start.18
  265.4 3.2 copy-start.21
  265.5 3.2 copy-start.22
  265.5 3.2 copy-start.23
  317.3 0.7 copy-start.17
  318.0 2.7 copy-start.10
  319.3 1.6 copy-start.11
  320.8 2.4 copy-start.12
  323.2 2.8 copy-start.4
  323.2 2.8 copy-start.1
  326.0 2.7 copy-start.6
  517.2 45.6 %all-to-all-start.2 = ((f32[128,15,384]{2,1,0:T(8,128)}), f32[128,15,384]{2,1,0:T(8,128)}, u32[]{:S(2)}, u32[]{:S(2)}) async-start(f32[128,15,384]{2,1,0:T(8,128)} %maximum_select_fusion.1), calls=%async_computation.2 | async-start | bytes 6291456 | tf_op jit(solution)/shard_map/all_to_all | solution.py:156
  525.8 8.5 %copy-start.2 = (f32[32,96,2,96]{3,2,1,0:T(2,128)S(1)}, f32[32,96,2,96]{3,2,1,0:T(2,128)}, u32[]{:S(2)}) copy-start(f32[32,96,2,96]{3,2,1,0:T(2,128)} %reshape_reshape.3) | copy-start | bytes 7077892
  525.8 8.5 %copy-start.5 = (f32[32,96,96]{2,1,0:T(8,128)S(1)}, f32[32,96,96]{2,1,0:T(8,128)}, u32[]{:S(2)}) copy-start(f32[32,96,96]{2,1,0:T(8,128)} %copy-done.4) | copy-start | bytes 3538948
  525.8 8.5 %copy-start.7 = (f32[32,96,96]{2,1,0:T(8,128)S(1)}, f32[32,96,96]{2,1,0:T(8,128)}, u32[]{:S(2)}) copy-start(f32[32,96,96]{2,1,0:T(8,128)} %copy-done.6) | copy-start | bytes 3538948
  600.0 4.4 copy-start.9
  600.3 4.1 copy-start.8
  611.2 3.8 copy-start.3
where the time goes:
time: 630 us; the launch traced here: 620 us
  local copies, waits for them, and re-layouts  477 us (76%)
  matrix products  48.4 us (8%)
  starting transfers between devices  31.4 us (5%)
  other arithmetic  29.5 us (5%)
  waiting for transfers between devices  29.1 us (5%)
    gather x4, local copies, waits for them, and re-layouts, serve(): col_re = state[slot, :, pig]  163 us
    gather x4, local copies, waits for them, and re-layouts, serve(): col_im = state[slot, :, pig + width]  157 us
    gather x2, local copies, waits for them, and re-layouts, neighbours(): picked = incoming[flat_target, jnp.minimum(ask_rank, capacity - 1)]  58.7 us
    gather x4, local copies, waits for them, and re-layouts, serve(): rows = state[slot, pig, :]  43.6 us
    all_to_all x2, waiting for transfers between devices, neighbours(): lax.all_to_all(serve(state, lax.all_to_all(codes, 'ha', split_axis=0, con...  25.2 us
    all_to_all x2, starting transfers between devices, neighbours(): lax.all_to_all(serve(state, lax.all_to_all(codes, 'ha', split_axis=0, con...  19.9 us
    dot_general x2, matrix products, derivative(): jnp.einsum('aipj,jk->aipk', state.reshape(count, width, 2, width), hmat,...  19 us
    unnamed x55, local copies, waits for them, and re-layouts  16.7 us
  transfers between devices with their start and end apart: 3, of which 3 were waited for; matrix products, arithmetic and copies ran while one was open for 9% of the time, Pallas kernels for 0%

commit v1 on v0

v1 whole, which is shorter than its diff:
```python
import functools

import jax
import jax.numpy as jnp
from jax import lax
from jax.experimental import pallas as pl
from jax.experimental.pallas import tpu as pltpu
from jax.sharding import PartitionSpec as P

M = 96
K = 40
A = 32
N = 128
Q = K * A
LIST = 192
C = 15
WIDE = 512
PIECES = 3 * C + 1
TAG = 96
HALF = 0.05
STEP = 0.1

f32, bf16, i32 = jnp.float32, jnp.bfloat16, jnp.int32
VMEM = pl.BlockSpec(memory_space=pltpu.VMEM)
SMEM = pl.BlockSpec(memory_space=pltpu.SMEM)


def iota(shape, axis):
    return lax.broadcasted_iota(i32, shape, axis)


def dot(a, b):
    return jnp.dot(a, b, preferred_element_type=f32)


def split(x):
    high = x.astype(bf16)
    return high, (x - high.astype(f32)).astype(bf16)


def pick(ones, x):
    high, low = split(x)
    return dot(ones, high) + dot(ones, low)


def spread(x, ones):
    high, low = split(x)
    return dot(high, ones) + dot(low, ones)


def onehot(mask):
    return jnp.where(mask, 1.0, 0.0).astype(bf16)


def widen(o0, o1, o2):
    lane = iota(o0.shape, 1)
    keep = lane < M
    t1 = pltpu.roll(jnp.where(lane >= 96, o0, o1), 32, 1)
    t2 = pltpu.roll(jnp.where(lane >= 64, o1, o2), 64, 1)
    t3 = pltpu.roll(o2, 96, 1)
    return [jnp.where(keep, t, 0.0) for t in (o0, t1, t2, t3)]


def narrow(t0, t1, t2, t3):
    lane = iota(t0.shape, 1)
    r1, r2, r3 = pltpu.roll(t1, 96, 1), pltpu.roll(t2, 64, 1), pltpu.roll(t3, 32, 1)
    return jnp.where(lane < 96, t0, r1), jnp.where(lane < 64, r1, r2), jnp.where(lane < 32, r2, r3)


def tile(x, j):
    return x[:, j * 128 : (j + 1) * 128]


def both(ref):
    return jnp.concatenate([ref[0], ref[1]], axis=1)


def pigment_columns(pig):
    lane = iota((1, 128), 1)
    at = jnp.full((1, 128), -1, i32)
    for k in range(K):
        at = jnp.where(lane == k, pig[k], at)
        at = jnp.where(lane == K + k, pig[k] + 128, at)
    return jnp.where(iota((256, 128), 0) == at, 1.0, 0.0)


def plan(links, coef, listed, slots):
    before = onehot(iota((256, 256), 0) < iota((256, 256), 1))
    device = iota((N, 256), 0)
    carry = jnp.zeros((N, 1), f32)
    order = iota((LIST, 256), 0)
    total = [jnp.zeros((LIST, 256), f32) for _ in range(4)]
    for h in range(2):
        for t in range(Q // 256):
            span = pl.ds(t * 256, 256)
            link = links[h : h + 1, span]
            dest = lax.shift_right_arithmetic(link, 5)
            mine = dest == device
            ones = jnp.where(mine, 1.0, 0.0)
            count = dot(ones.astype(bf16), before) + carry
            carry = count[:, 255:256] + ones[:, 255:256]
            rank = jnp.sum(jnp.where(mine, count, 0.0), axis=0, keepdims=True)
            place = jnp.sum(count, axis=0, keepdims=True).astype(i32)
            place = jnp.where(link >= 0, place, -1)
            slot = rank * N + dest.astype(f32)
            mode = lax.shift_right_arithmetic(iota((1, 256), 1) + t * 256, 5)
            tag = (mode * A + (link & 31) + 1).astype(f32)
            here = order == place
            new = jnp.where(here, 1.0, 0.0)
            listed[:, span] = new if h == 0 else listed[:, span] + new
            total[0] += jnp.where(here, slot, 0.0)
            total[1] += jnp.where(here, tag, 0.0)
            if h == 0:
                total[2] += jnp.where(here, coef[0:1, span], 0.0)
                total[3] += jnp.where(here, coef[1:2, span], 0.0)
            else:
                total[2] += new
    lane = iota((LIST, 128), 1)
    out = jnp.zeros((LIST, 128), f32)
    for j in range(4):
        out = jnp.where(lane == j, jnp.sum(total[j], axis=1, keepdims=True), out)
    slots[...] = jnp.where((lane == 0) & (out[:, 1:2] == 0.0), -1.0, out)


def pack(state, pig, columns, listed, slots, table, work, send):
    work[...] = spread(both(state), columns.astype(bf16))
    for k in range(K):
        for h in range(2):
            rows = pl.ds(pl.multiple_of(pig[k] * A, A), A)
            table[h, pl.ds(k * A, A), :] = state[h, rows, :]
    blank = jnp.zeros((128 - M, 128), f32)
    for a in range(A):
        block = jnp.concatenate([work[pl.ds(a, M, stride=A), :], blank], axis=0).T
        table[2, pl.ds(a, K, stride=A), :] = block[0:K]
        table[3, pl.ds(a, K, stride=A), :] = block[K : 2 * K]
    message = pick(listed[...].astype(bf16), jnp.concatenate([table[j] for j in range(4)], axis=1))
    info = slots[...]
    sa, sb = info[:, 2:3], info[:, 3:4]
    x0, x1, x2, x3 = (tile(message, j) for j in range(4))
    x0, x1, x2, x3 = sa * x1 + sb * x0, sb * x1 - sa * x0, sb * x2 - sa * x3, sa * x2 + sb * x3
    x0 = jnp.where(iota((LIST, 128), 1) == TAG, info[:, 1:2], x0)
    message = jnp.concatenate([x0, x1, x2, x3], axis=1)
    high, low = split(message)
    goal = info.T[0:1, :].astype(i32)
    lane = iota((N, 128), 1)
    tags = jnp.zeros((N, 128), f32)
    for r in range(C):
        ones = onehot(iota((N, LIST), 0) + r * N == goal)
        part = dot(ones, high) + dot(ones, low)
        tags = jnp.where(lane == r, pltpu.roll(tile(part, 0), (r - TAG) % 128, 1), tags)
        for j, piece in enumerate(narrow(*(tile(part, j) for j in range(4)))):
            send[pl.ds(3 * r + j, N, stride=PIECES), :] = piece
    send[pl.ds(3 * C, N, stride=PIECES), :] = tags


def receive(got):
    tags = got[pl.ds(3 * C, N, stride=PIECES), :]
    across = tags.T
    before = onehot(iota((128, 128), 0) < iota((128, 128), 1))
    lane = iota((N, 128), 1)
    carry = jnp.zeros((1, 1), f32)
    order = iota((LIST, 128), 0)
    out = jnp.zeros((LIST, WIDE), f32)
    full = onehot(across[0:16, :] > 0.5)
    count = dot(full, before)
    for r in range(C):
        tag = across[r : r + 1, :]
        ones = jnp.where(tag > 0.5, 1.0, 0.0)
        place = jnp.where(tag > 0.5, (count[r : r + 1, :] + carry).astype(i32), -1)
        carry = carry + count[r : r + 1, 127:128] + ones[:, 127:128]
        t0, t1, t2, t3 = widen(*(got[pl.ds(3 * r + j, N, stride=PIECES), :] for j in range(3)))
        t0 = jnp.where(lane == TAG, pltpu.roll(tags, TAG - r, 1), t0)
        out = out + pick(onehot(order == place), jnp.concatenate([t0, t1, t2, t3], axis=1))
    return out


def put(message, pig, columns, dense, work, total):
    tag = message[:, 0:128].T[TAG : TAG + 1, :].astype(i32)
    clean = jnp.where((iota(message.shape, 1) & 127) < M, message, 0.0)
    placed = pick(onehot(iota((Q, message.shape[0]), 0) + 1 == tag), clean)
    for j in range(4):
        dense[j] = tile(placed, j)
    blank = jnp.zeros((128 - 2 * K, 128), f32)
    for a in range(A):
        rows = pl.ds(a, K, stride=A)
        block = jnp.concatenate([dense[2, rows, :], dense[3, rows, :], blank], axis=0).T
        work[pl.ds(a, M, stride=A), :] = block[0:M]
    added = spread(work[...], columns.T.astype(bf16))
    for h in range(2):
        total[h] += tile(added, h)
    for k in range(K):
        for h in range(2):
            rows = pl.ds(pl.multiple_of(pig[k] * A, A), A)
            total[h, rows, :] += dense[h, pl.ds(k * A, A), :]


def open_kernel(pig, links, coef, density, state, send, listed, slots, table, work):
    plan(links, coef, listed, slots)
    for m in range(M // 2):
        parts = widen(*(density[:, m * 384 + j * 128 : m * 384 + (j + 1) * 128] for j in range(3)))
        for j in range(2):
            for h in range(2):
                state[h, pl.ds((2 * m + j) * A, A), :] = parts[2 * j + h]
    pack(state, pig, pigment_columns(pig), listed, slots, table, work, send)


def commutator_kernel(section, field, steps, decay, hamiltonian, dipole, state, out, twice):
    h = hamiltonian[...] + field[steps[section]] * dipole[...]
    twice[...] = jnp.zeros((256, 256), f32)
    twice[0:M, 0:M] = h
    twice[128 : 128 + M, 128 : 128 + M] = h
    hh, hl = split(h)
    bh, bl = split(twice[...])

    def body(a, _):
        rows = pl.ds(a, M, stride=A)
        x = jnp.concatenate([state[0, rows, :], state[1, rows, :]], axis=1)
        xh, xl = split(x)
        left = dot(hh, xh) + dot(hl, xh) + dot(hh, xl)
        right = dot(xh, bh) + dot(xh, bl) + dot(xl, bh)
        d = left - right
        rate = decay[a]
        out[0, rows, :] = d[:, 128:256] - rate * x[:, 0:128]
        out[1, rows, :] = -d[:, 0:128] - rate * x[:, 128:256]
        return _

    lax.fori_loop(0, A, body, 0, unroll=4)


def middle_kernel(pig, got, state, rate, listed, slots, middle, send, dense, work):
    columns = pigment_columns(pig)
    message = receive(got)
    middle[...] = rate[...]
    put(message, pig, columns, dense, work, middle)
    middle[...] = state[...] + HALF * middle[...]
    pack(middle, pig, columns, listed, slots, dense, work, send)


def close_kernel(pig, got, state, rate, out, total, dense, work):
    message = receive(got)
    total[...] = rate[...]
    put(message, pig, pigment_columns(pig), dense, work, total)
    for m in range(M // 2):
        parts = []
        for j in range(2):
            rows = pl.ds((2 * m + j) * A, A)
            for half in range(2):
                parts.append(state[half, rows, :] + STEP * total[half, rows, :])
        for j, piece in enumerate(narrow(*parts)):
            out[:, m * 384 + j * 128 : m * 384 + (j + 1) * 128] = piece


def call(kernel, in_specs, outs, scratch):
    return pl.pallas_call(
        kernel,
        in_specs=in_specs,
        out_specs=[VMEM] * len(outs),
        out_shape=[jax.ShapeDtypeStruct(*o) for o in outs],
        scratch_shapes=[pltpu.VMEM(*s) for s in scratch],
        compiler_params=pltpu.CompilerParams(vmem_limit_bytes=48 * 1024 * 1024),
    )


def exchange(send):
    got = lax.all_to_all(
        send.reshape(N, 1, PIECES * 128), "ha", split_axis=0, concat_axis=0, tiled=True
    )
    return got.reshape(N * PIECES, 128)


def on_device(
    density,
    up_link,
    down_link,
    occupation,
    pigments,
    hamiltonian,
    dipole,
    damping_rates,
    coupling_re,
    coupling_im,
    field,
    pulse_steps,
):
    links = jnp.stack([up_link.T.reshape(Q), down_link.T.reshape(Q)])
    level = occupation.astype(f32)
    raised = level.T + 1.0
    coef = jnp.stack(
        [
            (raised * coupling_re[:, None]).reshape(Q),
            (raised * coupling_im[:, None]).reshape(Q),
        ]
    )
    decay = jnp.sum(level * damping_rates[None, :], axis=1)
    big = ((2, M * A, 128), f32)
    sent = ((N * PIECES, 128), f32)
    listing = [((LIST, Q), f32), ((LIST, 128), f32)]
    dense, work = ((4, Q, 128), f32), ((M * A, 128), f32)

    state, send, listed, slots = call(
        open_kernel, [SMEM, VMEM, VMEM, VMEM], [big, sent] + listing, [dense, work]
    )(pigments, links, coef, density)

    def commutator(section, x):
        return call(
            functools.partial(commutator_kernel, section),
            [SMEM, SMEM, SMEM, VMEM, VMEM, VMEM],
            [big],
            [((256, 256), f32)],
        )(field, pulse_steps, decay, hamiltonian, dipole, x)[0]

    got = exchange(send)
    rate = commutator(0, state)
    middle, send = call(
        middle_kernel, [SMEM] + [VMEM] * 5, [big, sent], [dense, work]
    )(pigments, got, state, rate, listed, slots)
    got = exchange(send)
    rate = commutator(1, middle)
    out = call(
        close_kernel,
        [SMEM] + [VMEM] * 3,
        [((A, 2 * M * M), f32)],
        [big, dense, work],
    )(pigments, got, state, rate)
    return out[0]


def solution(mesh):
    rows = P("ha", None)
    return jax.shard_map(
        on_device,
        mesh=mesh,
        in_specs=(rows, rows, rows, rows) + (P(),) * 8,
        out_specs=rows,
        check_vma=False,
    )
```

time: 630 us -> 142 us (0.23); the launches traced: 620 us -> 141 us
  local copies, waits for them, and re-layouts: 477 us -> 7.73 us
  Pallas kernels: 0 us -> 59.7 us
  matrix products: 48.4 us -> 0 us
  other arithmetic: 29.5 us -> 0.89 us
  waiting for transfers between devices: 29.1 us -> 54.9 us
  starting transfers between devices: 31.4 us -> 18 us
    gather x14 -> x0, local copies, waits for them, and re-layouts: 423 us -> none  [the longest x4 163 us: serve(): col_re = state[slot, :, pig]]
    pallas_call x0 -> x5, Pallas kernels: none -> 59.7 us  [the longest x2 21.2 us: commutator(): call(functools.partial(commutator_kernel, section), [SMEM, SMEM, SMEM, VM...]
    dot_general x12 -> x0, matrix products: 48.4 us -> none  [the longest x2 19 us: derivative(): jnp.einsum('aipj,jk->aipk', state.reshape(count, width, 2, width), hmat,...]
    all_to_all x3 -> x2, waiting for transfers between devices: 29.1 us -> 54.9 us  [exchange(): lax.all_to_all(send.reshape(N, 1, PIECES * 128), 'ha', split_axis=0, conc...]
    select_n x4 -> x0, other arithmetic: 18.7 us -> none  [the longest x2 9.91 us: neighbours(): jnp.where(flat_valid[:, None], picked, jnp.float32(0.0))]
    all_to_all x3 -> x2, starting transfers between devices: 31.4 us -> 18 us  [exchange(): lax.all_to_all(send.reshape(N, 1, PIECES * 128), 'ha', split_axis=0, conc...]
    concatenate x9 -> x0, local copies, waits for them, and re-layouts: 11.2 us -> none  [the longest x3 10.3 us: derivative(): return jnp.concatenate([d_re, d_im], axis=-1) - decay * state]
    unnamed x55 -> x20, local copies, waits for them, and re-layouts: 16.7 us -> 5.66 us
  transfers between devices with their start and end apart: 3 -> 2, of which waited for: 3 -> 2; matrix products, arithmetic and copies ran while one was open for 9% -> 0% of each run, Pallas kernels for 0% -> 15%
where the time goes in v1:
time: 142 us; the launch traced here: 141 us
  Pallas kernels  59.7 us (42%)
  waiting for transfers between devices  54.9 us (39%)
  starting transfers between devices  18 us (13%)
  local copies, waits for them, and re-layouts  7.73 us (5%)
    all_to_all x2, waiting for transfers between devices, exchange(): lax.all_to_all(send.reshape(N, 1, PIECES * 128), 'ha', split_axis=0, conc...  54.9 us
    pallas_call x2, Pallas kernels, commutator(): call(functools.partial(commutator_kernel, section), [SMEM, SMEM, SMEM, VM...  21.2 us
    all_to_all x2, starting transfers between devices, exchange(): lax.all_to_all(send.reshape(N, 1, PIECES * 128), 'ha', split_axis=0, conc...  18 us
    pallas_call x1, Pallas kernels, on_device(): call(middle_kernel, [SMEM] + [VMEM] * 5, [big, sent], [dense, work])  17.8 us
    pallas_call x1, Pallas kernels, on_device(): call(close_kernel, [SMEM] + [VMEM] * 3, [((A, 2 * M * M), f32)], [big, de...  10.5 us
    pallas_call x1, Pallas kernels, on_device(): call(open_kernel, [SMEM, VMEM, VMEM, VMEM], [big, sent] + listing, [dense...  10.1 us
    unnamed x20, local copies, waits for them, and re-layouts  5.66 us
  transfers between devices with their start and end apart: 2, of which 2 were waited for; matrix products, arithmetic and copies ran while one was open for 0% of the time, Pallas kernels for 15%

profile of v1, /device:TPU:1, one launch (start us, length us, event | category | flops | bytes accessed | tf_op | source)
XLA Modules:
  0.0 141.3 jit_solution(15744871304346186506)
XLA Ops:
  0.0 0.8 copy.21
  0.8 0.1 stack_reshape.12
  0.9 0.8 copy.22
  1.7 0.1 stack_reshape.13
  1.8 0.9 multiply_reduce_fusion
  2.6 0.1 copy.24
  2.7 0.1 stack_reshape.15
  2.8 0.1 copy.23
  2.8 0.1 stack_reshape.14
  3.0 0.0 copy-start.3
  3.0 1.7 %copy-done.3 = f32[32,18432]{1,0:T(8,128)S(1)} copy-done((f32[32,18432]{1,0:T(8,128)S(1)}, f32[32,18432]{1,0:T(8,128)}, u32[]{:S(2)}) %copy-start.3) | copy-done | bytes 2359320
  4.6 0.0 copy-start.6
  4.7 0.7 copy-done.6
  5.3 10.1 %shard_map.118 = (f32[2,3072,128]{2,1,0:T(8,128)}, f32[5888,128]{1,0:T(8,128)}, f32[192,1280]{1,0:T(8,128)S(1)}, f32[192,128]{1,0:T(8,128)S(1)}) custom-call(s32[40]{0:T(128)S(1)} %copy-done.6, s32[2,1280]{1,0:T(2,128)S(1)} %pad_add_fusion.links, f32[2,1280]{1,0:T(2,128)S(1)} %pad_maximum_fusion.coef, f32[32,18432]{1,0:T(8,128)S(1)} %copy-done.3), custom_call_target="tpu_custom_call" | custom-call | tf_op jit(solution)/shard_map/pallas_call | solution.py:300
  15.4 0.0 copy-start.4
  15.4 0.0 copy-start.5
  15.4 0.0 copy-start.8
  15.4 0.0 copy-start.9
  15.4 11.9 %all-to-all-start = ((f32[128,1,5888]{2,1,0:T(1,128)}), f32[128,1,5888]{2,1,0:T(1,128)}, u32[]{:S(2)}, u32[]{:S(2)}) async-start(f32[128,1,5888]{2,1,0:T(1,128)} %bitcast.10), calls=%async_computation | async-start | bytes 6029312 | tf_op jit(solution)/shard_map/all_to_all | solution.py:265
  27.3 0.0 copy-done.4
  27.4 0.0 copy-done.5
  27.4 0.0 copy-done.8
  27.4 0.0 copy-done.9
  27.4 0.0 copy-start.7
  27.4 10.6 %shard_map.119.rate = f32[2,3072,128]{2,1,0:T(8,128)S(1)} custom-call(f32[64]{0:T(128)S(1)} %copy-done.8, s32[2]{0:T(128)S(1)} %copy-done.9, f32[32]{0:T(128)S(1)} %get-tuple-element.17.decay, f32[96,96]{1,0:T(8,128)S(1)} %copy-done.4, f32[96,96]{1,0:T(8,128)S(1)} %copy-done.5, f32[2,3072,128]{2,1,0:T(8,128)} %get-tuple-element.12.state), custom_call_target="tpu_custom_call" | custom-call | tf_op jit(solution)/shard_map/pallas_call | solution.py:305
  38.0 0.0 copy-start.2
  38.0 1.7 %copy-done.2 = f32[2,3072,128]{2,1,0:T(8,128)} copy-done((f32[2,3072,128]{2,1,0:T(8,128)}, f32[2,3072,128]{2,1,0:T(8,128)S(1)}, u32[]{:S(2)}) %copy-start.2) | copy-done | bytes 3145752
  39.7 27.3 %all-to-all-done = f32[128,1,5888]{2,1,0:T(1,128)} async-done(((f32[128,1,5888]{2,1,0:T(1,128)}), f32[128,1,5888]{2,1,0:T(1,128)}, u32[]{:S(2)}, u32[]{:S(2)}) %all-to-all-start) | async-done | bytes 3014688 | tf_op jit(solution)/shard_map/all_to_all | solution.py:265
  67.0 0.0 copy-done.7
  67.0 17.8 %shard_map.120 = (f32[2,3072,128]{2,1,0:T(8,128)}, f32[5888,128]{1,0:T(8,128)}) custom-call(s32[40]{0:T(128)S(1)} %copy-done.7, f32[5888,128]{1,0:T(8,128)} %bitcast.5.got, f32[2,3072,128]{2,1,0:T(8,128)} %get-tuple-element.12.state, f32[2,3072,128]{2,1,0:T(8,128)} %copy-done.2, f32[192,1280]{1,0:T(8,128)S(1)} %get-tuple-element.13.listed, ...), custom_call_target="tpu_custom_call" | custom-call | tf_op jit(solution)/shard_map/pallas_call | solution.py:314
  84.8 6.1 %all-to-all-start.1 = ((f32[128,1,5888]{2,1,0:T(1,128)}), f32[128,1,5888]{2,1,0:T(1,128)}, u32[]{:S(2)}, u32[]{:S(2)}) async-start(f32[128,1,5888]{2,1,0:T(1,128)} %bitcast.6), calls=%async_computation.1 | async-start | bytes 6029312 | tf_op jit(solution)/shard_map/all_to_all | solution.py:265
  90.9 0.0 copy-start
  90.9 10.6 %shard_map.121.rate = f32[2,3072,128]{2,1,0:T(8,128)S(1)} custom-call(f32[64]{0:T(128)S(1)} %copy-done.8, s32[2]{0:T(128)S(1)} %copy-done.9, f32[32]{0:T(128)S(1)} %get-tuple-element.17.decay, f32[96,96]{1,0:T(8,128)S(1)} %copy-done.4, f32[96,96]{1,0:T(8,128)S(1)} %copy-done.5, f32[2,3072,128]{2,1,0:T(8,128)} %get-tuple-element.16.state), custom_call_target="tpu_custom_call" | custom-call | tf_op jit(solution)/shard_map/pallas_call | solution.py:305
  101.5 0.0 copy-start.1
  101.5 1.7 %copy-done.1 = f32[2,3072,128]{2,1,0:T(8,128)} copy-done((f32[2,3072,128]{2,1,0:T(8,128)}, f32[2,3072,128]{2,1,0:T(8,128)S(1)}, u32[]{:S(2)}) %copy-start.1) | copy-done | bytes 3145752
  103.2 27.5 %all-to-all-done.1 = f32[128,1,5888]{2,1,0:T(1,128)} async-done(((f32[128,1,5888]{2,1,0:T(1,128)}), f32[128,1,5888]{2,1,0:T(1,128)}, u32[]{:S(2)}, u32[]{:S(2)}) %all-to-all-start.1) | async-done | bytes 3014688 | tf_op jit(solution)/shard_map/all_to_all | solution.py:265
  130.7 0.0 copy-done
  130.7 10.5 %shard_map.122 = f32[32,18432]{1,0:T(8,128)} custom-call(s32[40]{0:T(128)S(1)} %copy-done.7, f32[5888,128]{1,0:T(8,128)} %bitcast.7.got, f32[2,3072,128]{2,1,0:T(8,128)S(1)} %copy-done, f32[2,3072,128]{2,1,0:T(8,128)} %copy-done.1), custom_call_target="tpu_custom_call" | custom-call | tf_op jit(solution)/shard_map/pallas_call | solution.py:319
  (2 shorter events, 0.0 us)
Async XLA Ops:
  3.0 1.7 %copy-start.3 = (f32[32,18432]{1,0:T(8,128)S(1)}, f32[32,18432]{1,0:T(8,128)}, u32[]{:S(2)}) copy-start(f32[32,18432]{1,0:T(8,128)} %density.1) | copy-start | bytes 7077892
  4.6 0.7 copy-start.6
  15.4 11.9 %copy-start.4 = (f32[96,96]{1,0:T(8,128)S(1)}, f32[96,96]{1,0:T(8,128)}, u32[]{:S(2)}) copy-start(f32[96,96]{1,0:T(8,128)} %hamiltonian.3) | copy-start | bytes 110596
  15.4 11.9 %copy-start.5 = (f32[96,96]{1,0:T(8,128)S(1)}, f32[96,96]{1,0:T(8,128)}, u32[]{:S(2)}) copy-start(f32[96,96]{1,0:T(8,128)} %dipole.3) | copy-start | bytes 110596
  15.4 11.9 %copy-start.8 = (f32[64]{0:T(128)S(1)}, f32[64]{0:T(128)}, u32[]{:S(2)}) copy-start(f32[64]{0:T(128)} %field.3) | copy-start | bytes 772
  15.4 11.9 %copy-start.9 = (s32[2]{0:T(128)S(1)}, s32[2]{0:T(128)}, u32[]{:S(2)}) copy-start(s32[2]{0:T(128)} %steps.3) | copy-start | bytes 28
  15.4 51.6 %all-to-all-start = ((f32[128,1,5888]{2,1,0:T(1,128)}), f32[128,1,5888]{2,1,0:T(1,128)}, u32[]{:S(2)}, u32[]{:S(2)}) async-start(f32[128,1,5888]{2,1,0:T(1,128)} %bitcast.10), calls=%async_computation | async-start | bytes 6029312 | tf_op jit(solution)/shard_map/all_to_all | solution.py:265
  27.4 39.6 %copy-start.7 = (s32[40]{0:T(128)S(1)}, s32[40]{0:T(128)}, u32[]{:S(2)}) copy-start(s32[40]{0:T(128)} %pig.5) | copy-start | bytes 484
  38.0 1.7 %copy-start.2 = (f32[2,3072,128]{2,1,0:T(8,128)}, f32[2,3072,128]{2,1,0:T(8,128)S(1)}, u32[]{:S(2)}) copy-start(f32[2,3072,128]{2,1,0:T(8,128)S(1)} %shard_map.119.rate) | copy-start | bytes 9437188
  84.8 45.9 %all-to-all-start.1 = ((f32[128,1,5888]{2,1,0:T(1,128)}), f32[128,1,5888]{2,1,0:T(1,128)}, u32[]{:S(2)}, u32[]{:S(2)}) async-start(f32[128,1,5888]{2,1,0:T(1,128)} %bitcast.6), calls=%async_computation.1 | async-start | bytes 6029312 | tf_op jit(solution)/shard_map/all_to_all | solution.py:265
  90.9 39.8 %copy-start = (f32[2,3072,128]{2,1,0:T(8,128)S(1)}, f32[2,3072,128]{2,1,0:T(8,128)}, u32[]{:S(2)}) copy-start(f32[2,3072,128]{2,1,0:T(8,128)} %get-tuple-element.12.state) | copy-start | bytes 9437188
  101.5 1.7 %copy-start.1 = (f32[2,3072,128]{2,1,0:T(8,128)}, f32[2,3072,128]{2,1,0:T(8,128)S(1)}, u32[]{:S(2)}) copy-start(f32[2,3072,128]{2,1,0:T(8,128)S(1)} %shard_map.121.rate) | copy-start | bytes 9437188
